TPU v7x, 256 devices: a whole 4x4x8 slice. The times are simulated.
256 devices in a mesh: dp: 64 (over z, x, core), mp: 4 (over y).
Axes of the slice: x: 4, y: 4, z: 8, core: 2. Of those that a mesh axis runs over, the one named last changes fastest.
Arguments:
- queries: bfloat16 [131072, 2048], P('dp', 'mp'), may hold values from -102 to 102
- cotangent: bfloat16 [131072, 2048], P('dp', 'mp'), may hold values from -12 to 12
- passages: bfloat16 [128, 128, 4096], P('dp', None, 'mp'), may hold values from -6 to 6
- w_kv: bfloat16 [4096, 2, 2048], P(None, None, 'mp'), may hold values from -0.09375 to 0.09375
- neighbour_ids: int32 [64, 32, 2], P('dp'), may hold values from 0 to 127, as said below
- passage_slot: int32 [128], replicated, may hold values from 0 to 127, as said below
Outputs:
- grad_passages: bfloat16 [128, 128, 4096], P('dp', None, 'mp')
Inputs may be any that keep to these rules, and one draw needn't show every extreme that they name: `passage_slot`: a permutation of the slots. The slots passage_slot[neighbour_ids] of the 64 neighbours of one sequence, divided by 2, take every value 0 to 63 exactly 1 times; a passage may be named more than once.
All inputs are finite; a program needn't handle non-finite values.
Results may differ from a plain program's by a relative error of at most 0.028.
The roundings to bfloat16 on the way count: a program that leaves them out, or rounds other values in their place, can miss the bound.
Values may be sent and summed in bfloat16 or wider, within the bound.
No kernel may reach another device: no remote copies, remote signals or barrier semaphores. Data moves between devices by JAX's collectives and lax.ppermute only.
A program may use at most 192 MiB of HBM per device.

v0:
```python
import math

import jax
import jax.numpy as jnp
from jax import lax
from jax.sharding import PartitionSpec as P

HEAD_DIM = 128
GROUP = 64


def project_rows(w_kv, shard_piece):
    return jnp.einsum("pnd,dkw->pnkw", shard_piece, w_kv, preferred_element_type=jnp.float32)


def per_device(queries, cotangent, passages, w_kv, neighbour_ids, passage_slot):
    enc_count, near_len, part_width = passages.shape
    kv_width = w_kv.shape[2]
    head_count = kv_width // HEAD_DIM
    seq_tokens = queries.shape[0]
    group_count = seq_tokens // GROUP
    ref_count = 2 * group_count
    peer_count = lax.axis_size("dp")
    per_peer = ref_count // peer_count
    score_scale = 1.0 / math.sqrt(HEAD_DIM)
    encoded = project_rows(w_kv, lax.all_gather(passages, "mp", axis=2, tiled=True)).astype(
        jnp.bfloat16
    )
    slot_rows = passage_slot[neighbour_ids.reshape(-1)]
    owner_shard = slot_rows // enc_count
    local_slot = slot_rows % enc_count
    owner_hits = (owner_shard[:, None] == jnp.arange(peer_count)[None, :]).astype(jnp.int32)
    earlier = jnp.cumsum(owner_hits, axis=0) - owner_hits
    rank_within = jnp.sum(earlier * owner_hits, axis=1)
    position = owner_shard * per_peer + rank_within
    request = (
        jnp.zeros((ref_count,), jnp.int32)
        .at[position]
        .set(local_slot)
        .reshape(peer_count, per_peer)
    )
    wanted = lax.all_to_all(request, "dp", split_axis=0, concat_axis=0, tiled=True).reshape(-1)
    owned_hits = (wanted[:, None] == jnp.arange(enc_count)[None, :]).astype(jnp.float32)
    grad_blocks = cotangent.reshape(group_count, GROUP, head_count, HEAD_DIM)
    source_ref = (
        jnp.zeros((ref_count,), jnp.int32).at[position].set(jnp.arange(ref_count, dtype=jnp.int32))
    )
    group_at_slot = source_ref // 2
    group_queries = queries.reshape(group_count, GROUP, kv_width)
    queued = group_queries[group_at_slot]
    visiting = lax.all_to_all(
        queued.reshape(peer_count, per_peer, GROUP, kv_width),
        "dp",
        split_axis=0,
        concat_axis=0,
        tiled=True,
    ).reshape(ref_count, GROUP, head_count, HEAD_DIM)
    local_kv = encoded[wanted].reshape(ref_count, near_len, 2, head_count, HEAD_DIM)
    key_rows = local_kv[:, :, 0]
    value_rows = local_kv[:, :, 1]
    scores = (
        jnp.einsum("rqhe,rkhe->rhqk", visiting, key_rows, preferred_element_type=jnp.float32)
        * score_scale
    )
    peak_score = jnp.max(scores, axis=3)
    weights_un = jnp.exp(scores - peak_score[..., None])
    mass_part = jnp.sum(weights_un, axis=3)
    partial_value = jnp.einsum(
        "rhqk,rkhe->rqhe", weights_un, value_rows.astype(jnp.float32)
    ).reshape(peer_count, per_peer, GROUP, kv_width)
    back_sums, back_peak, back_mass = (
        lax.all_to_all(partial_value, "dp", split_axis=0, concat_axis=0, tiled=True),
        lax.all_to_all(
            peak_score.reshape(peer_count, per_peer, head_count, GROUP),
            "dp",
            split_axis=0,
            concat_axis=0,
            tiled=True,
        ),
        lax.all_to_all(
            mass_part.reshape(peer_count, per_peer, head_count, GROUP),
            "dp",
            split_axis=0,
            concat_axis=0,
            tiled=True,
        ),
    )
    mine_sums = back_sums.reshape(ref_count, GROUP, kv_width)[position].reshape(
        group_count, 2, GROUP, head_count, HEAD_DIM
    )
    mine_peak = back_peak.reshape(ref_count, head_count, GROUP)[position].reshape(
        group_count, 2, head_count, GROUP
    )
    mine_mass = back_mass.reshape(ref_count, head_count, GROUP)[position].reshape(
        group_count, 2, head_count, GROUP
    )
    joint_peak = jnp.max(mine_peak, axis=1, keepdims=True)
    factor = jnp.exp(mine_peak - joint_peak)
    total_mass = jnp.sum(mine_mass * factor, axis=1)
    log_total = joint_peak[:, 0] + jnp.log(total_mass)
    weighted = jnp.sum(mine_sums * jnp.transpose(factor, (0, 1, 3, 2))[..., None], axis=1)
    attended = weighted / jnp.transpose(total_mass, (0, 2, 1))[..., None]
    delta_rows = jnp.transpose(
        jnp.sum(grad_blocks.astype(jnp.float32) * attended, axis=3), (0, 2, 1)
    )
    group_grads = cotangent.reshape(group_count, GROUP, kv_width)
    grad_queue = group_grads[group_at_slot]
    total_queue = log_total[group_at_slot]
    delta_queue = delta_rows[group_at_slot]
    grad_visit = lax.all_to_all(
        grad_queue.reshape(peer_count, per_peer, GROUP, kv_width),
        "dp",
        split_axis=0,
        concat_axis=0,
        tiled=True,
    ).reshape(ref_count, GROUP, head_count, HEAD_DIM)
    total_visit, delta_visit = (
        lax.all_to_all(
            total_queue.reshape(peer_count, per_peer, head_count, GROUP),
            "dp",
            split_axis=0,
            concat_axis=0,
            tiled=True,
        ),
        lax.all_to_all(
            delta_queue.reshape(peer_count, per_peer, head_count, GROUP),
            "dp",
            split_axis=0,
            concat_axis=0,
            tiled=True,
        ),
    )
    total_visit = total_visit.reshape(ref_count, head_count, GROUP)
    delta_visit = delta_visit.reshape(ref_count, head_count, GROUP)
    softmax_w = jnp.exp(scores - total_visit[..., None])
    grad_prob = jnp.einsum(
        "rqhe,rkhe->rhqk", grad_visit, value_rows, preferred_element_type=jnp.float32
    )
    dscore = (softmax_w * (grad_prob - delta_visit[..., None])).astype(jnp.bfloat16)
    probs_low = softmax_w.astype(jnp.bfloat16)
    slot_mask = jnp.transpose(owned_hits).astype(jnp.bfloat16)[:, :, None, None, None]
    dscore_slot = dscore[None] * slot_mask
    probs_slot = probs_low[None] * slot_mask
    grad_keys = (
        jnp.einsum("prhqk,rqhe->pkhe", dscore_slot, visiting, preferred_element_type=jnp.float32)
        * score_scale
    )
    grad_values = jnp.einsum(
        "prhqk,rqhe->pkhe", probs_slot, grad_visit, preferred_element_type=jnp.float32
    )
    grad_kv = (
        jnp.stack([grad_keys, grad_values], axis=2)
        .reshape(enc_count, near_len, 2, kv_width)
        .astype(jnp.bfloat16)
    )
    head_term = jnp.einsum("pnkw,dkw->pnd", grad_kv, w_kv, preferred_element_type=jnp.float32)
    return lax.psum_scatter(head_term.astype(jnp.bfloat16), "mp", scatter_dimension=2, tiled=True)


def solution(mesh):
    placed = (
        P("dp", "mp"),
        P("dp", "mp"),
        P("dp", None, "mp"),
        P(None, None, "mp"),
        P("dp", None, None),
        P(),
    )
    return jax.shard_map(
        per_device, mesh=mesh, in_specs=placed, out_specs=P("dp", None, "mp"), check_vma=False
    )
```

profile of v0, /device:TPU:1, one launch (start us, length us, event | category | flops | bytes accessed | tf_op | source)
XLA Modules:
  0.0 649.2 jit_solution(7533065640140127377)
XLA Ops:
  10.9 13.0 %all-to-all-start.1 = ((s32[64,1,1]{2,1,0:T(1,128)}), s32[64,1,1]{2,1,0:T(1,128)S(1)}, u32[]{:S(2)}, u32[]{:S(2)}) async-start(s32[64,1,1]{2,1,0:T(1,128)} %copy.59), calls=%async_computation.1 | async-start | bytes 65536 | tf_op jit(solution)/shard_map/all_to_all | solution.py:42
  40.9 35.3 %all-gather.2.cloned.1.call-done = bf16[2,128,4096]{2,1,0:T(8,128)(2,1)} async-done(((bf16[2,128,1024]{2,1,0:T(8,128)(2,1)}), bf16[2,128,4096]{2,1,0:T(8,128)(2,1)}) %all-gather.2.cloned.1.call-update) | async-done | bytes 2097168 | tf_op jit(solution)/shard_map/all_gather | solution.py:26
  82.6 7.3 %gather_fusion.2 = bf16[64,128,2,512]{3,1,2,0:T(8,128)(2,1)} fusion(bf16[2,128,2,512]{3,1,2,0:T(8,128)(2,1)S(1)} %fusion.37, s32[1024]{0:T(1024)S(1)} %pad_clamp_fusion.1), kind=kCustom, calls=%fused_computation.2 | custom fusion | bytes 33554688 | tf_op jit(solution)/shard_map/gather | solution.py:58
  89.9 23.7 %reshape.228 = bf16[64,128,2,4,128]{4,3,1,2,0:T(4,128)(2,1)} reshape(bf16[64,128,2,512]{3,1,2,0:T(8,128)(2,1)} %gather_fusion.2) | data formatting | bytes 33554432 | tf_op jit(solution)/shard_map/reshape | solution.py:58
  113.6 15.9 %fusion.93 = (bf16[64,128,1,4,128]{4,3,1,2,0:T(4,128)(2,1)}, bf16[64,128,1,4,128]{4,3,1,2,0:T(4,128)(2,1)}) fusion(bf16[64,128,2,4,128]{4,3,1,2,0:T(4,128)(2,1)} %reshape.228), kind=kLoop, calls=%fused_computation.104 | loop fusion | bytes 33554432 | tf_op jit(solution)/shard_map/slice | solution.py:60
  140.5 13.8 %multiply_reduce_fusion.1 = (f32[64,4,64]{2,1,0:T(4,128)S(1)}, f32[64,4,64,128]{3,2,1,0:T(8,128)}) fusion(bf16[64,128,1,4,128]{4,3,1,2,0:T(4,128)(2,1)} %get-tuple-element.6, bf16[64,64,4,128]{3,2,1,0:T(4,128)(2,1)} %reshape.227), kind=kOutput, calls=%fused_computation.33 | convolution fusion | flops 541048832 | bytes 21037056 | tf_op jit(solution)/shard_map/rqhe,rkhe->rhqk/dot_general | solution.py:62
  154.4 7.0 %fusion.10 = f32[64,4,64]{2,1,0:T(4,128)S(1)} fusion(f32[64,4,64,128]{3,2,1,0:T(8,128)} %get-tuple-element.12, f32[64,4,64]{2,1,0:T(4,128)S(1)} %get-tuple-element.11), kind=kLoop, calls=%fused_computation.27 | loop fusion | flops 6275072 | bytes 8519680 | tf_op jit(solution)/shard_map/reduce_sum | solution.py:67
  162.2 7.0 %all-to-all-start.3 = ((f32[64,1,256]{2,1,0:T(1,128)}), f32[64,1,256]{2,1,0:T(1,128)S(1)}, u32[]{:S(2)}, u32[]{:S(2)}) async-start(f32[64,1,256]{2,1,0:T(1,128)} %reshape.352), calls=%async_computation.3 | async-start | bytes 131072 | tf_op jit(solution)/shard_map/all_to_all | solution.py:80
  169.9 9.3 %all-to-all-done.3 = f32[64,1,256]{2,1,0:T(1,128)S(1)} async-done(((f32[64,1,256]{2,1,0:T(1,128)}), f32[64,1,256]{2,1,0:T(1,128)S(1)}, u32[]{:S(2)}, u32[]{:S(2)}) %all-to-all-start.3) | async-done | bytes 65568 | tf_op jit(solution)/shard_map/all_to_all | solution.py:80
  186.9 7.4 %all-to-all-done.2 = f32[64,1,256]{2,1,0:T(1,128)S(1)} async-done(((f32[64,1,256]{2,1,0:T(1,128)}), f32[64,1,256]{2,1,0:T(1,128)S(1)}, u32[]{:S(2)}, u32[]{:S(2)}) %all-to-all-start.2) | async-done | bytes 65568 | tf_op jit(solution)/shard_map/all_to_all | solution.py:73
  204.9 89.4 %all-to-all-done.5 = bf16[64,1,64,512]{3,2,1,0:T(8,128)(2,1)} async-done(((bf16[64,1,64,512]{3,2,1,0:T(8,128)(2,1)}), bf16[64,1,64,512]{3,2,1,0:T(8,128)(2,1)}, u32[]{:S(2)}, u32[]{:S(2)}) %all-to-all-start.5) | async-done | bytes 4194336 | tf_op jit(solution)/shard_map/all_to_all | solution.py:110
  301.3 9.5 %fusion.33 = f32[64,64,4,128]{3,1,2,0:T(8,128)} fusion(f32[64,4,64,128]{3,2,1,0:T(8,128)} %get-tuple-element.12, f32[64,4,64]{2,1,0:T(4,128)S(1)} %get-tuple-element.11, bf16[64,128,1,4,128]{4,3,1,2,0:T(4,128)(2,1)} %get-tuple-element.5), kind=kOutput, calls=%fused_computation.48 | convolution fusion | flops 541065216 | bytes 25231360 | tf_op jit(solution)/shard_map/rhqk,rkhe->rqhe/dot_general | solution.py:68
  310.8 14.6 %copy.65 = f32[64,64,4,128]{3,2,1,0:T(4,128)} copy(f32[64,64,4,128]{3,1,2,0:T(8,128)} %fusion.33) | data formatting | bytes 16777216 | tf_op jit(solution)/shard_map/rhqk,rkhe->rqhe/transpose | solution.py:68
  325.4 10.3 %reshape.239 = f32[64,1,64,512]{3,2,0,1:T(8,128)} reshape(f32[64,64,4,128]{3,2,1,0:T(4,128)} %copy.65) | data formatting | bytes 16777216 | tf_op jit(solution)/shard_map/reshape | solution.py:70
  335.7 10.8 %all-to-all-start.6 = ((f32[64,1,64,512]{3,2,1,0:T(8,128)}), f32[64,1,64,512]{3,2,1,0:T(8,128)}, u32[]{:S(2)}, u32[]{:S(2)}) async-start(f32[64,1,64,512]{3,2,1,0:T(8,128)} %bitcast.131), calls=%async_computation.6 | async-start | bytes 16777216 | tf_op jit(solution)/shard_map/all_to_all | solution.py:72
  369.0 159.8 %all-to-all-done.6 = f32[64,1,64,512]{3,2,1,0:T(8,128)} async-done(((f32[64,1,64,512]{3,2,1,0:T(8,128)}), f32[64,1,64,512]{3,2,1,0:T(8,128)}, u32[]{:S(2)}, u32[]{:S(2)}) %all-to-all-start.6) | async-done | bytes 8388640 | tf_op jit(solution)/shard_map/all_to_all | solution.py:72
  528.8 7.7 %gather_fusion.7 = f32[64,64,512]{2,1,0:T(8,128)} fusion(f32[64,64,512]{2,1,0:T(8,128)} %bitcast.27, s32[1024]{0:T(1024)S(1)} %pad_clamp_fusion), kind=kCustom, calls=%fused_computation.7 | custom fusion | bytes 16777472 | tf_op jit(solution)/shard_map/gather | solution.py:88
  536.5 9.9 %reshape.241 = f32[32,2,64,4,128]{4,3,2,1,0:T(4,128)} reshape(f32[64,64,512]{2,1,0:T(8,128)} %gather_fusion.7) | data formatting | bytes 16777216 | tf_op jit(solution)/shard_map/reshape | solution.py:88
  546.4 9.7 %multiply_reduce_fusion = f32[32,64,4,128]{3,2,1,0:T(4,128)S(1)} fusion(f32[32,2,64,4,128]{4,3,2,1,0:T(4,128)} %reshape.241, f32[32,2,64,4]{3,2,1,0:T(8,128)S(1)} %copy.67), kind=kLoop, calls=%fused_computation.23 | loop fusion | flops 3145728 | bytes 12648448 | tf_op jit(solution)/shard_map/reduce_sum | solution.py:101
  562.8 10.0 %all-to-all-start.7 = ((f32[64,1,256]{2,1,0:T(1,128)}), f32[64,1,256]{2,1,0:T(1,128)S(1)}, u32[]{:S(2)}, u32[]{:S(2)}) async-start(f32[64,1,256]{2,1,0:T(1,128)} %reshape.356), calls=%async_computation.7 | async-start | bytes 131072 | tf_op jit(solution)/shard_map/all_to_all | solution.py:125
  573.0 8.4 %fusion.67 = bf16[2,128,4,128]{1,3,0,2:T(8,128)(2,1)S(1)} fusion(bf16[64,4,64,128]{3,0,2,1:T(8,128)(2,1)} %copy.74, bf16[2,64]{1,0:T(2,128)(2,1)S(1)} %fusion.83, bf16[64,64,4,128,1]{3,2,1,0,4:T(4,128)(2,1)} %bitcast.136), kind=kOutput, calls=%fused_computation.56 | convolution fusion | flops 1090650112 | bytes 8651008 | tf_op jit(solution)/shard_map/prhqk,rqhe->pkhe/dot_general | solution.py:148
  583.7 10.0 %multiply_convert_fusion = bf16[64,4,64,128]{3,2,1,0:T(8,128)(2,1)S(1)} fusion(f32[64,4,64,128]{3,2,1,0:T(8,128)} %get-tuple-element.12, f32[64,4,64]{2,1,0:T(4,128)S(1)} %bitcast.152, f32[64,4,64]{2,1,0:T(4,128)S(1)} %bitcast.146, bf16[64,128,1,4,128]{4,3,1,2,0:T(4,128)(2,1)} %get-tuple-element.5, bf16[64,64,4,128]{3,2,1,0:T(4,128)(2,1)} %reshape.238), kind=kOutput, calls=%fused_computation.22 | convolution fusion | flops 547356672 | bytes 25296896 | tf_op jit(solution)/shard_map/rqhe,rkhe->rhqk/dot_general | solution.py:136
  602.5 7.2 %fusion.19 = bf16[2,128,4096]{2,1,0:T(8,128)(2,1)} fusion(bf16[4096,2,512]{2,1,0:T(2,128)(2,1)} %param.9, bf16[2,128,1,512]{3,1,2,0:T(8,128)(2,1)S(1)} %copy.78, bf16[2,128,1,512]{3,1,2,0:T(8,128)(2,1)S(1)} %copy.77), kind=kOutput, calls=%fused_computation.35 | convolution fusion | flops 2148794368 | bytes 11010048 | tf_op jit(solution)/shard_map/pnkw,dkw->pnd/dot_general | solution.py:156
  609.8 32.3 %reduce-scatter.2.cloned.1.call-done = bf16[2,128,1024]{2,1,0:T(8,128)(2,1)} async-done(((bf16[2,128,4096]{2,1,0:T(8,128)(2,1)}), bf16[2,128,1024]{2,1,0:T(8,128)(2,1)}) %reduce-scatter.2.cloned.1.call-update) | async-done | bytes 524304 | tf_op jit(solution)/shard_map/reduce_scatter | solution.py:157
  (81 shorter events, 105.6 us)
Async XLA Ops:
  6.5 18.2 %copy-start = (bf16[2048,512]{1,0:T(8,128)(2,1)S(1)}, bf16[2048,512]{1,0:T(8,128)(2,1)}, u32[]{:S(2)}) copy-start(bf16[2048,512]{1,0:T(8,128)(2,1)} %param.6) | copy-start | bytes 6291460
  10.9 22.3 %all-to-all-start.1 = ((s32[64,1,1]{2,1,0:T(1,128)}), s32[64,1,1]{2,1,0:T(1,128)S(1)}, u32[]{:S(2)}, u32[]{:S(2)}) async-start(s32[64,1,1]{2,1,0:T(1,128)} %copy.59), calls=%async_computation.1 | async-start | bytes 65536 | tf_op jit(solution)/shard_map/all_to_all | solution.py:42
  33.2 100.4 %all-to-all-start = ((bf16[64,1,64,512]{3,2,1,0:T(8,128)(2,1)}), bf16[64,1,64,512]{3,2,1,0:T(8,128)(2,1)}, u32[]{:S(2)}, u32[]{:S(2)}) async-start(bf16[64,1,64,512]{3,2,1,0:T(8,128)(2,1)} %bitcast.134), calls=%async_computation | async-start | bytes 8388608 | tf_op jit(solution)/shard_map/all_to_all | solution.py:51
  38.9 37.3 %all-gather.2.cloned.1.call-start = ((), (), s32[]{:S(2)}) async-start(), calls=%async_computation.9 | async-start | bytes 2621440 | tf_op jit(solution)/shard_map/all_gather | solution.py:26
  154.3 29.8 %copy-start.2 = (bf16[2048,512]{1,0:T(8,128)(2,1)S(1)}, bf16[2048,512]{1,0:T(8,128)(2,1)}, u32[]{:S(2)}) copy-start(bf16[2048,512]{1,0:T(8,128)(2,1)} %param.7) | copy-start | bytes 6291460
  162.2 17.1 %all-to-all-start.3 = ((f32[64,1,256]{2,1,0:T(1,128)}), f32[64,1,256]{2,1,0:T(1,128)S(1)}, u32[]{:S(2)}, u32[]{:S(2)}) async-start(f32[64,1,256]{2,1,0:T(1,128)} %reshape.352), calls=%async_computation.3 | async-start | bytes 131072 | tf_op jit(solution)/shard_map/all_to_all | solution.py:80
  179.3 15.0 %all-to-all-start.2 = ((f32[64,1,256]{2,1,0:T(1,128)}), f32[64,1,256]{2,1,0:T(1,128)S(1)}, u32[]{:S(2)}, u32[]{:S(2)}) async-start(f32[64,1,256]{2,1,0:T(1,128)} %reshape.350), calls=%async_computation.2 | async-start | bytes 131072 | tf_op jit(solution)/shard_map/all_to_all | solution.py:73
  194.2 100.1 %all-to-all-start.5 = ((bf16[64,1,64,512]{3,2,1,0:T(8,128)(2,1)}), bf16[64,1,64,512]{3,2,1,0:T(8,128)(2,1)}, u32[]{:S(2)}, u32[]{:S(2)}) async-start(bf16[64,1,64,512]{3,2,1,0:T(8,128)(2,1)} %bitcast.135), calls=%async_computation.5 | async-start | bytes 8388608 | tf_op jit(solution)/shard_map/all_to_all | solution.py:110
  294.3 41.4 %all-to-all-start.4 = ((f32[64,1,256]{2,1,0:T(1,128)}), f32[64,1,256]{2,1,0:T(1,128)S(1)}, u32[]{:S(2)}, u32[]{:S(2)}) async-start(f32[64,1,256]{2,1,0:T(1,128)} %reshape.354), calls=%async_computation.4 | async-start | bytes 131072 | tf_op jit(solution)/shard_map/all_to_all | solution.py:118
  335.7 193.2 %all-to-all-start.6 = ((f32[64,1,64,512]{3,2,1,0:T(8,128)}), f32[64,1,64,512]{3,2,1,0:T(8,128)}, u32[]{:S(2)}, u32[]{:S(2)}) async-start(f32[64,1,64,512]{3,2,1,0:T(8,128)} %bitcast.131), calls=%async_computation.6 | async-start | bytes 16777216 | tf_op jit(solution)/shard_map/all_to_all | solution.py:72
  546.4 9.7 %copy-start.4 = (f32[32,64,4,128]{3,2,1,0:T(4,128)S(1)}, f32[32,64,4,128]{3,2,1,0:T(4,128)}, u32[]{:S(2)}) copy-start(f32[32,64,4,128]{3,2,1,0:T(4,128)} %reshape.243) | copy-start | bytes 12582916
  562.8 20.1 %all-to-all-start.7 = ((f32[64,1,256]{2,1,0:T(1,128)}), f32[64,1,256]{2,1,0:T(1,128)S(1)}, u32[]{:S(2)}, u32[]{:S(2)}) async-start(f32[64,1,256]{2,1,0:T(1,128)} %reshape.356), calls=%async_computation.7 | async-start | bytes 131072 | tf_op jit(solution)/shard_map/all_to_all | solution.py:125
  572.8 69.3 %reduce-scatter.2.cloned.1.call-start = ((), (), s32[]{:S(2)}) async-start(), calls=%async_computation.10 | async-start | bytes 2621440 | tf_op jit(solution)/shard_map/reduce_scatter | solution.py:157
  593.7 2.7 copy-start.3
  602.4 39.7 %copy-start.1 = (bf16[2048,512]{1,0:T(8,128)(2,1)S(1)}, bf16[2048,512]{1,0:T(8,128)(2,1)}, u32[]{:S(2)}) copy-start(bf16[2048,512]{1,0:T(8,128)(2,1)} %param.6) | copy-start | bytes 6291460
Sparse Core Ops, SparseCore 0:
  41.6 34.6 all-gather.1
  609.9 32.1 reduce-scatter.1
where the time goes:
time: 654 us; the launch traced here: 649 us
  waiting for transfers between devices  345 us (53%)
  local copies, waits for them, and re-layouts  132 us (20%)
  starting transfers between devices  64.2 us (10%)
  matrix products  61.1 us (9%)
  other arithmetic  32.3 us (5%)
  between operations  14.1 us (2%)
    all_to_all x1, waiting for transfers between devices, per_device(): lax.all_to_all(partial_value, 'dp', split_axis=0, concat_axis=0, tiled=True)  160 us
    all_to_all x1, waiting for transfers between devices, per_device(): lax.all_to_all(grad_queue.reshape(peer_count, per_peer, GROUP, kv_width),...  89.4 us
    all_gather x1, waiting for transfers between devices, per_device(): lax.all_gather(passages, 'mp', axis=2, tiled=True)  35.3 us
    reduce_scatter x1, waiting for transfers between devices, per_device(): lax.psum_scatter(head_term.astype(jnp.bfloat16), 'mp', scatter_dimension=...  32.3 us
    reshape x1, local copies, waits for them, and re-layouts, per_device(): encoded[wanted].reshape(ref_count, near_len, 2, head_count, HEAD_DIM)  23.7 us
    slice x1, local copies, waits for them, and re-layouts, per_device(): value_rows = local_kv[:, :, 1]  15.9 us
    transpose x1, local copies, waits for them, and re-layouts, per_device(): jnp.einsum('rhqk,rkhe->rqhe', weights_un, value_rows.astype(jnp.float32))  14.6 us
    dot_general x1, matrix products, per_device(): jnp.einsum('rqhe,rkhe->rhqk', visiting, key_rows, preferred_element_type=...  13.8 us
  transfers between devices with their start and end apart: 10, of which 9 were waited for; matrix products, arithmetic and copies ran while one was open for 20% of the time, Pallas kernels for 0%

commit v1 on v0

v1 whole, which is shorter than its diff:
```python
import math

import jax
import jax.numpy as jnp
from jax import lax
from jax.experimental import pallas as pl
from jax.experimental.pallas import tpu as pltpu
from jax.sharding import Mesh
from jax.sharding import PartitionSpec as P

HEAD_DIM = 128
GROUP = 64
NZ, NX, NC, NY = 8, 4, 2, 4
NLAYER = NX * NC
ENC = 2
NEAR = 128
LAYER = ("x", "c")
CHUNKS = ((0, 2), (2, 2))
BF16 = jnp.bfloat16
F32 = jnp.float32
NT = (((1,), (1,)), ((), ()))
NN = (((1,), (0,)), ((), ()))
SCALE = 1.0 / math.sqrt(HEAD_DIM)


def queue_kernel(ids, slot_of, q_ref, cot_ref, out_ref, group_at):
    dest = pl.program_id(0)

    @pl.when(dest == 0)
    def _():
        def place(ref, carry):
            group_at[slot_of[ids[ref]] // ENC] = ref // 2
            return carry

        lax.fori_loop(0, NZ * NLAYER, place, 0)

    for z in range(NZ):
        group = group_at[z * NLAYER + dest]
        out_ref[0, 0, z] = q_ref[group]
        out_ref[0, 1, z] = cot_ref[group]


def queue_groups(ids, slot_of, queries, cotangent, first, heads):
    groups = queries.shape[0]
    width = heads * HEAD_DIM
    at = first // heads
    source = pl.BlockSpec((groups, GROUP, width), lambda i, *_: (0, 0, at))
    return pl.pallas_call(
        queue_kernel,
        grid_spec=pltpu.PrefetchScalarGridSpec(
            num_scalar_prefetch=2,
            grid=(NLAYER,),
            in_specs=[source, source],
            out_specs=pl.BlockSpec((1, 2, NZ, GROUP, width), lambda i, *_: (i, 0, 0, 0, 0)),
            scratch_shapes=[pltpu.SMEM((NZ * NLAYER,), jnp.int32)],
        ),
        out_shape=jax.ShapeDtypeStruct((NLAYER, 2, NZ, GROUP, width), BF16),
        compiler_params=pltpu.CompilerParams(vmem_limit_bytes=24 * 1024 * 1024),
        cost_estimate=pl.CostEstimate(
            flops=0, bytes_accessed=3 * groups * GROUP * width * 4, transcendentals=0
        ),
        name="queue_groups",
    )(ids, slot_of, queries, cotangent)


def pick(both, second):
    return jnp.where(second, both[NEAR:], both[:NEAR])


def head_parts(visit_ref, kv_ref, head):
    cols = slice(head * HEAD_DIM, (head + 1) * HEAD_DIM)
    rows = NLAYER * GROUP
    q = visit_ref[:, 0, 0, :, cols].reshape(rows, HEAD_DIM)
    cot = visit_ref[:, 1, 0, :, cols].reshape(rows, HEAD_DIM)
    return q, cot, kv_ref[0, 0, :, cols], kv_ref[0, 1, :, cols]


def scores_of(q, cot, keys, values, second):
    score = lax.dot_general(keys, q, NT, preferred_element_type=F32)
    grad_prob = lax.dot_general(values, cot, NT, preferred_element_type=F32)
    return pick(score, second) * SCALE, pick(grad_prob, second)


def stats_kernel(heads, slot_ref, visit_ref, kv_ref, out_ref):
    z = pl.program_id(0)
    second = slot_ref[pl.ds(z, 1), :] == 1
    lse_rows, delta_rows = [], []
    for head in range(heads):
        score, grad_prob = scores_of(*head_parts(visit_ref, kv_ref, head), second)
        peak = jnp.max(score, axis=0, keepdims=True)
        weight = jnp.exp(score - peak)
        mass = jnp.sum(weight, axis=0, keepdims=True)
        lse_rows.append(peak + jnp.log(mass))
        delta_rows.append(jnp.sum(weight * grad_prob, axis=0, keepdims=True) / mass)
    for at, row in enumerate(lse_rows + delta_rows):
        out_ref[pl.ds(at * NZ + z, 1), :] = row


def visit_spec(width):
    return pl.BlockSpec((NLAYER, 2, 1, GROUP, width), lambda z, *_: (0, 0, z, 0, 0))


def kv_spec(width):
    return pl.BlockSpec((1, 2, ENC * NEAR, width), lambda z, *_: (z, 0, 0, 0))


def whole(shape):
    return pl.BlockSpec(shape, lambda z, *_: (0,) * len(shape))


def attention_cost(heads, matmuls):
    products = NZ * heads * NLAYER * GROUP * ENC * NEAR * HEAD_DIM
    moved = NZ * heads * HEAD_DIM * 2 * (2 * NLAYER * GROUP + 2 * ENC * NEAR)
    return pl.CostEstimate(
        flops=2 * matmuls * products,
        bytes_accessed=moved,
        transcendentals=NZ * heads * NLAYER * GROUP * NEAR,
    )


def partial_stats(slot_lanes, visit, kv, heads):
    width = heads * HEAD_DIM
    lanes = NLAYER * GROUP
    return pl.pallas_call(
        lambda *refs: stats_kernel(heads, *refs),
        grid=(NZ,),
        in_specs=[whole((NZ, lanes)), visit_spec(width), kv_spec(width)],
        out_specs=whole((NZ * 2 * heads, lanes)),
        out_shape=jax.ShapeDtypeStruct((NZ * 2 * heads, lanes), F32),
        compiler_params=pltpu.CompilerParams(vmem_limit_bytes=32 * 1024 * 1024),
        cost_estimate=attention_cost(heads, 2),
        name="partial_stats",
    )(slot_lanes, visit, kv)


def grads_kernel(heads, partner, slot_ref, visit_ref, kv_ref, own_ref, all_ref, out_ref):
    z = pl.program_id(0)
    second = slot_ref[pl.ds(z, 1), :] == 1
    low_lane = lax.broadcasted_iota(jnp.int32, (NZ, 2 * GROUP), 1) < GROUP
    z_row = lax.broadcasted_iota(jnp.int32, (NZ, 2 * GROUP), 0)
    places = [partner[z * NLAYER + source] for source in range(NLAYER)]

    def other(row):
        pieces = []
        for pair in range(NLAYER // 2):
            cols = slice(pair * 2 * GROUP, (pair + 1) * 2 * GROUP)
            low, high = (
                jnp.where(
                    z_row == where % NZ, all_ref[where // NZ, row * NZ : (row + 1) * NZ, cols], 0.0
                )
                for where in places[2 * pair : 2 * pair + 2]
            )
            pieces.append(jnp.sum(jnp.where(low_lane, low, high), axis=0, keepdims=True))
        return jnp.concatenate(pieces, axis=1)

    def mine(row):
        return own_ref[pl.ds(row * NZ + z, 1), :]

    totals, deltas = [], []
    for head in range(heads):
        lse_mine, lse_other = mine(head), other(head)
        top = jnp.maximum(lse_mine, lse_other)
        total = top + jnp.log(jnp.exp(lse_mine - top) + jnp.exp(lse_other - top))
        totals.append(total)
        deltas.append(
            mine(heads + head) * jnp.exp(lse_mine - total)
            + other(heads + head) * jnp.exp(lse_other - total)
        )
    for head in range(heads):
        cols = slice(head * HEAD_DIM, (head + 1) * HEAD_DIM)
        q, cot, keys, values = head_parts(visit_ref, kv_ref, head)
        score, grad_prob = scores_of(q, cot, keys, values, second)
        probs = jnp.exp(score - totals[head])
        dscore = probs * (grad_prob - deltas[head])
        for at, (weight, rows_of) in enumerate(((dscore, q), (probs, cot))):
            spread = jnp.concatenate(
                [jnp.where(second, 0.0, weight), jnp.where(second, weight, 0.0)], axis=0
            ).astype(BF16)
            grad = lax.dot_general(spread, rows_of, NN, preferred_element_type=F32)
            if at == 0:
                grad = grad * SCALE
            out_ref[0, at, :, cols] = grad.astype(BF16)


def visit_grads(partner, slot_lanes, visit, kv, own, gathered, heads):
    width = heads * HEAD_DIM
    lanes = NLAYER * GROUP
    rows = NZ * 2 * heads
    return pl.pallas_call(
        lambda *refs: grads_kernel(heads, *refs),
        grid_spec=pltpu.PrefetchScalarGridSpec(
            num_scalar_prefetch=1,
            grid=(NZ,),
            in_specs=[
                whole((NZ, lanes)),
                visit_spec(width),
                kv_spec(width),
                whole((rows, lanes)),
                whole((NLAYER, rows, lanes)),
            ],
            out_specs=kv_spec(width),
        ),
        out_shape=jax.ShapeDtypeStruct((NZ, 2, ENC * NEAR, width), BF16),
        compiler_params=pltpu.CompilerParams(vmem_limit_bytes=32 * 1024 * 1024),
        cost_estimate=attention_cost(heads, 4),
        name="visit_grads",
    )(partner, slot_lanes, visit, kv, own, gathered)


def per_device(queries, cotangent, passages, w_kv, neighbour_ids, passage_slot):
    enc_count, near_len, part_width = passages.shape
    seq_tokens, part_cols = queries.shape
    groups = seq_tokens // GROUP
    ids = neighbour_ids.reshape(-1)
    queries = queries.reshape(groups, GROUP, part_cols)
    cotangent = cotangent.reshape(groups, GROUP, part_cols)

    visits = [
        lax.all_to_all(
            queue_groups(ids, passage_slot, queries, cotangent, first, heads),
            LAYER,
            split_axis=0,
            concat_axis=0,
            tiled=True,
        )
        for first, heads in CHUNKS
    ]

    encoded = lax.all_gather(passages, "y", axis=2, tiled=True).reshape(enc_count * near_len, -1)

    layer_ids = lax.all_gather(ids, LAYER, axis=0, tiled=False)
    layer_slots = passage_slot[layer_ids]
    owner = layer_slots // ENC
    partner_owner = owner.reshape(NLAYER, groups, 2)[:, :, ::-1].reshape(NLAYER, -1)
    here = lax.axis_index("x") * NC + lax.axis_index("c")
    targets = jnp.arange(NZ, dtype=jnp.int32) * NLAYER + here
    hits = (owner[None] == targets[:, None, None]).astype(jnp.int32)
    local_slot = jnp.sum(hits * (layer_slots % ENC)[None], axis=2)
    partner = jnp.sum(hits * partner_owner[None], axis=2)
    partner = ((partner % NLAYER) * NZ + partner // NLAYER).reshape(-1)
    slot_lanes = jnp.repeat(local_slot, GROUP, axis=1)

    grads = []
    for (first, heads), visit in zip(CHUNKS, visits, strict=True):
        cols = slice(first * HEAD_DIM, (first + heads) * HEAD_DIM)
        kv_here = jnp.einsum(
            "nd,dkw->knw", encoded, w_kv[:, :, cols], preferred_element_type=F32
        ).astype(BF16)
        kv = lax.all_gather(kv_here, "z", axis=0, tiled=False)
        own = partial_stats(slot_lanes, visit, kv, heads)
        gathered = lax.all_gather(own, LAYER, axis=0, tiled=False)
        grad = visit_grads(partner, slot_lanes, visit, kv, own, gathered, heads)
        grads.append(lax.psum_scatter(grad, "z", scatter_dimension=0, tiled=False))
    grad_kv = jnp.concatenate(grads, axis=2)
    head_term = jnp.einsum("knw,dkw->nd", grad_kv, w_kv, preferred_element_type=F32).astype(BF16)
    out = lax.psum_scatter(head_term, "y", scatter_dimension=1, tiled=True)
    return out.reshape(enc_count, near_len, part_width)


def solution(mesh):
    fine = Mesh(mesh.devices.reshape(NZ, NX, NC, NY), ("z", "x", "c", "y"))
    dp = ("z", "x", "c")
    placed = (
        P(dp, "y"),
        P(dp, "y"),
        P(dp, None, "y"),
        P(None, None, "y"),
        P(dp, None, None),
        P(),
    )
    return jax.shard_map(
        per_device, mesh=fine, in_specs=placed, out_specs=P(dp, None, "y"), check_vma=False
    )
```

time: 654 us -> 328 us (0.50)
  waiting for transfers between devices: 345 us -> 114 us
  blocking collectives: 0 us -> 109 us
  local copies, waits for them, and re-layouts: 132 us -> 25 us
  starting transfers between devices: 64.2 us -> 10.1 us
  matrix products: 61.1 us -> 15.8 us
  Pallas kernels: 0 us -> 38.6 us
  other arithmetic: 32.3 us -> 0.54 us
    all_to_all x8 -> x2, waiting for transfers between devices: 277 us -> 0.01 us  [per_device(): lax.all_to_all(queue_groups(ids, passage_slot, queries, cotangent, first,...]
    all_gather x0 -> x3, blocking collectives: none -> 109 us  [the longest x2 62.1 us: per_device(): gathered = lax.all_gather(own, LAYER, axis=0, tiled=False)]
    reshape x6 -> x2, local copies, waits for them, and re-layouts: 57.9 us -> 0.18 us  [the longest x1 0.1 us: per_device(): ids = neighbour_ids.reshape(-1)]
    all_to_all x8 -> x2, starting transfers between devices: 63.8 us -> 9.75 us  [per_device(): lax.all_to_all(queue_groups(ids, passage_slot, queries, cotangent, first,...]
    reduce_scatter x1 -> x3, waiting for transfers between devices: 32.3 us -> 82.5 us  [the longest x2 46.9 us: per_device(): grads.append(lax.psum_scatter(grad, 'z', scatter_dimension=0, tiled=False))]
    dot_general x7 -> x3, matrix products: 61.1 us -> 15.8 us  [the longest x2 8.5 us: per_device(): jnp.einsum('nd,dkw->knw', encoded, w_kv[:, :, cols], preferred_element_ty...]
    pallas_call x0 -> x6, Pallas kernels: none -> 38.6 us  [the longest x2 21.2 us: visit_grads(): pl.pallas_call(lambda *refs: grads_kernel(heads, *refs), grid_spec=pltpu....]
    reduce_sum x4 -> x1, other arithmetic: 21.7 us -> 0.41 us  [per_device(): local_slot = jnp.sum(hits * (layer_slots % ENC)[None], axis=2)]
  transfers between devices with their start and end apart: 10 -> 8, of which waited for: 9 -> 4; matrix products, arithmetic and copies ran while one was open for 20% -> 6% of each run, Pallas kernels for 0% -> 12%
where the time goes in v1:
time: 328 us; the launch traced here: 327 us
  waiting for transfers between devices  114 us (35%)
  blocking collectives  109 us (33%)
  Pallas kernels  38.6 us (12%)
  local copies, waits for them, and re-layouts  25 us (8%)
  matrix products  15.8 us (5%)
  between operations  13.7 us (4%)
  starting transfers between devices  10.1 us (3%)
    all_gather x2, blocking collectives, per_device(): gathered = lax.all_gather(own, LAYER, axis=0, tiled=False)  62.1 us
    all_gather x1, blocking collectives, per_device(): layer_ids = lax.all_gather(ids, LAYER, axis=0, tiled=False)  47.2 us
    reduce_scatter x2, waiting for transfers between devices, per_device(): grads.append(lax.psum_scatter(grad, 'z', scatter_dimension=0, tiled=False))  46.9 us
    reduce_scatter x1, waiting for transfers between devices, per_device(): out = lax.psum_scatter(head_term, 'y', scatter_dimension=1, tiled=True)  35.6 us
    all_gather x1, waiting for transfers between devices, per_device(): lax.all_gather(passages, 'y', axis=2, tiled=True)  30.6 us
    pallas_call x2, Pallas kernels, visit_grads(): pl.pallas_call(lambda *refs: grads_kernel(heads, *refs), grid_spec=pltpu....  21.2 us
    pallas_call x2, Pallas kernels, partial_stats(): pl.pallas_call(lambda *refs: stats_kernel(heads, *refs), grid=(NZ,), in_s...  13.3 us
    unnamed x20, local copies, waits for them, and re-layouts  10.5 us
  transfers between devices with their start and end apart: 8, of which 4 were waited for; matrix products, arithmetic and copies ran while one was open for 6% of the time, Pallas kernels for 12%

profile of v1, /device:TPU:1, one launch (start us, length us, event | category | flops | bytes accessed | tf_op | source)
XLA Modules:
  0.0 327.0 jit_solution(4097470970831341555)
XLA Ops:
  7.3 8.5 %fusion.36 = (bf16[4096,2,256]{2,1,0:T(2,128)(2,1)}, bf16[4096,2,256]{2,1,0:T(2,128)(2,1)}) fusion(bf16[4096,2,512]{2,1,0:T(2,128)(2,1)} %param.9), kind=kLoop, calls=%fused_computation.46 | loop fusion | bytes 16777216 | tf_op jit(solution)/shard_map/slice | solution.py:247
  15.8 30.6 %all-gather.9.cloned.1.call-done = bf16[2,128,4096]{2,1,0:T(8,128)(2,1)} async-done(((bf16[2,128,1024]{2,1,0:T(8,128)(2,1)}), bf16[2,128,4096]{2,1,0:T(8,128)(2,1)}) %all-gather.9.cloned.1.call-update) | async-done | bytes 2097168 | tf_op jit(solution)/shard_map/all_gather | solution.py:229
  46.4 4.3 %fusion.21 = bf16[2,256,256]{1,2,0:T(8,128)(2,1)S(1)} fusion(bf16[256,4096,1]{1,0,2:T(8,128)(2,1)} %bitcast.36, bf16[4096,2,256]{2,1,0:T(2,128)(2,1)} %get-tuple-element.7), kind=kOutput, calls=%fused_computation.12 | convolution fusion | flops 1073872896 | bytes 6553600 | tf_op jit(solution)/shard_map/nd,dkw->knw/dot_general | solution.py:246
  53.4 2.1 queue_groups.2
  55.5 1.9 copy-done.1
  57.4 5.1 %all-to-all-start = ((bf16[8,2,8,64,256]{4,3,2,1,0:T(8,128)(2,1)}), bf16[8,2,8,64,256]{4,3,2,1,0:T(8,128)(2,1)}, u32[]{:S(2)}, u32[]{:S(2)}) async-start(bf16[8,2,8,64,256]{4,3,2,1,0:T(8,128)(2,1)} %copy-done.1), calls=%async_computation | async-start | bytes 8388608 | tf_op jit(solution)/shard_map/all_to_all | solution.py:219
  62.5 4.2 %fusion.18 = bf16[2,256,256]{1,2,0:T(8,128)(2,1)S(1)} fusion(bf16[256,4096,1]{1,0,2:T(8,128)(2,1)} %bitcast.37, bf16[4096,2,256]{2,1,0:T(2,128)(2,1)} %get-tuple-element.8), kind=kOutput, calls=%fused_computation.11 | convolution fusion | flops 1073872896 | bytes 6553600 | tf_op jit(solution)/shard_map/nd,dkw->knw/dot_general | solution.py:246
  67.7 47.2 %all-gather.4 = s32[8,1,64]{2,1,0:T(1,128)S(1)} all-gather(s32[1,1,64]{2,1,0:T(1,128)S(1)} %reshape.79), channel_id=1, replica_groups=mesh['z'=8,'x'=4,'c'=2,'y'=4] {'x','c'}, dimensions={0}, use_global_device_ids=true | all-gather | bytes 2304 | tf_op jit(solution)/shard_map/all_gather | solution.py:231
  115.0 3.3 %gather_fusion = s32[512]{0:T(512)S(1)} fusion(s32[128]{0:T(128)S(1)} %copy-done, s32[1024]{0:T(1024)S(1)} %pad_clamp_fusion), kind=kCustom, calls=%fused_computation | custom fusion | bytes 6144 | tf_op jit(solution)/shard_map/gather | solution.py:232
  118.6 1.6 copy-done.5
  120.2 2.1 queue_groups.3
  122.2 2.0 copy-done.2
  125.4 4.6 %all-to-all-start.1 = ((bf16[8,2,8,64,256]{4,3,2,1,0:T(8,128)(2,1)}), bf16[8,2,8,64,256]{4,3,2,1,0:T(8,128)(2,1)}, u32[]{:S(2)}, u32[]{:S(2)}) async-start(bf16[8,2,8,64,256]{4,3,2,1,0:T(8,128)(2,1)} %copy-done.2), calls=%async_computation.2 | async-start | bytes 8388608 | tf_op jit(solution)/shard_map/all_to_all | solution.py:219
  130.1 1.6 copy-done.7
  131.7 6.7 %partial_stats.2.refs_4_ = f32[32,512]{1,0:T(8,128)S(1)} custom-call(s32[8,512]{1,0:T(8,128)S(1)} %reshape.58.refs_0_.refs_1_, bf16[8,2,8,64,256]{4,3,2,1,0:T(8,128)(2,1)} %all-to-all-done.refs_1_.refs_2_, bf16[8,2,256,256]{3,2,1,0:T(8,128)(2,1)S(1)} %bitcast.30), custom_call_target="tpu_custom_call" | custom-call | flops 1073741824 | bytes 6291456 | tf_op jit(solution)/shard_map/partial_stats/pallas_call | solution.py:124
  138.4 49.0 %all-gather.1 = f32[256,512]{1,0:T(8,128)S(1)} all-gather(f32[32,512]{1,0:T(8,128)S(1)} %partial_stats.2.refs_4_), channel_id=3, replica_groups=mesh['z'=8,'x'=4,'c'=2,'y'=4] {'x','c'}, dimensions={0}, use_global_device_ids=true | all-gather | bytes 589824 | tf_op jit(solution)/shard_map/all_gather | solution.py:251
  187.4 10.6 %visit_grads.2 = bf16[8,2,256,256]{3,2,1,0:T(8,128)(2,1)} custom-call(s32[64]{0:T(128)S(1)} %fusion.34.refs_0_, s32[8,512]{1,0:T(8,128)S(1)} %reshape.58.refs_0_.refs_1_, bf16[8,2,8,64,256]{4,3,2,1,0:T(8,128)(2,1)} %all-to-all-done.refs_1_.refs_2_, bf16[8,2,256,256]{3,2,1,0:T(8,128)(2,1)S(1)} %bitcast.31, f32[32,512]{1,0:T(8,128)S(1)} %partial_stats.2.refs_4_, ...), custom_call_target="tpu_custom_call" | custom-call | flops 2147483648 | bytes 6291456 | tf_op jit(solution)/shard_map/visit_grads/pallas_call | solution.py:189
  199.6 6.7 %partial_stats.3.refs_4_ = f32[32,512]{1,0:T(8,128)S(1)} custom-call(s32[8,512]{1,0:T(8,128)S(1)} %reshape.58.refs_0_.refs_1_, bf16[8,2,8,64,256]{4,3,2,1,0:T(8,128)(2,1)} %all-to-all-done.1.refs_1_.refs_2_, bf16[8,2,256,256]{3,2,1,0:T(8,128)(2,1)S(1)} %bitcast.28), custom_call_target="tpu_custom_call" | custom-call | flops 1073741824 | bytes 6291456 | tf_op jit(solution)/shard_map/partial_stats/pallas_call | solution.py:124
  206.3 13.1 %all-gather.3 = f32[256,512]{1,0:T(8,128)S(1)} all-gather(f32[32,512]{1,0:T(8,128)S(1)} %partial_stats.3.refs_4_), channel_id=5, replica_groups=mesh['z'=8,'x'=4,'c'=2,'y'=4] {'x','c'}, dimensions={0}, use_global_device_ids=true | all-gather | bytes 589824 | tf_op jit(solution)/shard_map/all_gather | solution.py:251
  219.4 10.6 %visit_grads.3 = bf16[8,2,256,256]{3,2,1,0:T(8,128)(2,1)} custom-call(s32[64]{0:T(128)S(1)} %fusion.34.refs_0_, s32[8,512]{1,0:T(8,128)S(1)} %reshape.58.refs_0_.refs_1_, bf16[8,2,8,64,256]{4,3,2,1,0:T(8,128)(2,1)} %all-to-all-done.1.refs_1_.refs_2_, bf16[8,2,256,256]{3,2,1,0:T(8,128)(2,1)S(1)} %bitcast.29, f32[32,512]{1,0:T(8,128)S(1)} %partial_stats.3.refs_4_, ...), custom_call_target="tpu_custom_call" | custom-call | flops 2147483648 | bytes 6291456 | tf_op jit(solution)/shard_map/visit_grads/pallas_call | solution.py:189
  230.3 3.9 %reduce-scatter.4.cloned.1.call-done = bf16[1,2,256,256]{3,2,1,0:T(8,128)(2,1)} async-done(((bf16[8,2,256,256]{3,2,1,0:T(8,128)(2,1)}), bf16[1,2,256,256]{3,2,1,0:T(8,128)(2,1)}) %reduce-scatter.4.cloned.1.call-update) | async-done | bytes 262160 | tf_op jit(solution)/shard_map/reduce_scatter | solution.py:253
  234.2 43.0 %reduce-scatter.6.cloned.1.call-done = bf16[1,2,256,256]{3,2,1,0:T(8,128)(2,1)} async-done(((bf16[8,2,256,256]{3,2,1,0:T(8,128)(2,1)}), bf16[1,2,256,256]{3,2,1,0:T(8,128)(2,1)}) %reduce-scatter.6.cloned.1.call-update) | async-done | bytes 262160 | tf_op jit(solution)/shard_map/reduce_scatter | solution.py:253
  277.2 7.3 %fusion.5 = bf16[256,4096]{1,0:T(8,128)(2,1)} fusion(bf16[4096,2,512]{2,1,0:T(2,128)(2,1)} %param.9, bf16[2,256,256]{2,1,0:T(8,128)(2,1)} %bitcast.39, bf16[2,256,256]{2,1,0:T(8,128)(2,1)} %bitcast.38), kind=kOutput, calls=%fused_computation.4 | convolution fusion | flops 2149580800 | bytes 11010048 | tf_op jit(solution)/shard_map/knw,dkw->nd/dot_general | solution.py:255
  284.5 35.6 %reduce-scatter.8.cloned.1.call-done = bf16[256,1024]{1,0:T(8,128)(2,1)} async-done(((bf16[256,4096]{1,0:T(8,128)(2,1)}), bf16[256,1024]{1,0:T(8,128)(2,1)}) %reduce-scatter.8.cloned.1.call-update) | async-done | bytes 524304 | tf_op jit(solution)/shard_map/reduce_scatter | solution.py:256
  (51 shorter events, 7.8 us)
Async XLA Ops:
  6.5 39.9 %all-gather.9.cloned.1.call-start = ((), (), s32[]{:S(2)}) async-start(), calls=%async_computation.5 | async-start | bytes 2621440 | tf_op jit(solution)/shard_map/all_gather | solution.py:229
  7.3 122.8 %all-gather.11.cloned.1.call-start = ((), (), s32[]{:S(2)}) async-start(), calls=%async_computation.9 | async-start | bytes 2359296 | tf_op jit(solution)/shard_map/all_gather | solution.py:249
  46.4 5.2 %copy-start.8 = (s32[1,32,2]{1,2,0:T(2,128)S(1)}, s32[1,32,2]{1,2,0:T(2,128)}, u32[]{:S(2)}) copy-start(s32[1,32,2]{1,2,0:T(2,128)} %param.10) | copy-start | bytes 772
  46.4 5.4 %copy-start = (s32[128]{0:T(128)S(1)}, s32[128]{0:T(128)}, u32[]{:S(2)}) copy-start(s32[128]{0:T(128)} %slot_of.3) | copy-start | bytes 1540
  46.4 5.4 %copy-start.3 = (bf16[2048,512]{1,0:T(8,128)(2,1)S(1)}, bf16[2048,512]{1,0:T(8,128)(2,1)}, u32[]{:S(2)}) copy-start(bf16[2048,512]{1,0:T(8,128)(2,1)} %param.6) | copy-start | bytes 6291460
  51.8 1.6 copy-start.4
  55.5 1.9 copy-start.1
  57.4 68.0 %all-to-all-start = ((bf16[8,2,8,64,256]{4,3,2,1,0:T(8,128)(2,1)}), bf16[8,2,8,64,256]{4,3,2,1,0:T(8,128)(2,1)}, u32[]{:S(2)}, u32[]{:S(2)}) async-start(bf16[8,2,8,64,256]{4,3,2,1,0:T(8,128)(2,1)} %copy-done.1), calls=%async_computation | async-start | bytes 8388608 | tf_op jit(solution)/shard_map/all_to_all | solution.py:219
  62.5 135.5 %all-gather.13.cloned.1.call-start = ((), (), s32[]{:S(2)}) async-start(), calls=%async_computation.10 | async-start | bytes 2359296 | tf_op jit(solution)/shard_map/all_gather | solution.py:249
  118.5 1.6 copy-start.5
  122.2 2.0 copy-start.2
  125.4 72.6 %all-to-all-start.1 = ((bf16[8,2,8,64,256]{4,3,2,1,0:T(8,128)(2,1)}), bf16[8,2,8,64,256]{4,3,2,1,0:T(8,128)(2,1)}, u32[]{:S(2)}, u32[]{:S(2)}) async-start(bf16[8,2,8,64,256]{4,3,2,1,0:T(8,128)(2,1)} %copy-done.2), calls=%async_computation.2 | async-start | bytes 8388608 | tf_op jit(solution)/shard_map/all_to_all | solution.py:219
  130.1 104.1 %reduce-scatter.4.cloned.1.call-start = ((), (), s32[]{:S(2)}) async-start(), calls=%async_computation.6 | async-start | bytes 2359296 | tf_op jit(solution)/shard_map/reduce_scatter | solution.py:253
  130.1 1.6 copy-start.7
  198.0 79.2 %reduce-scatter.6.cloned.1.call-start = ((), (), s32[]{:S(2)}) async-start(), calls=%async_computation.7 | async-start | bytes 2359296 | tf_op jit(solution)/shard_map/reduce_scatter | solution.py:253
  198.1 1.6 copy-start.6
  230.1 90.0 %reduce-scatter.8.cloned.1.call-start = ((), (), s32[]{:S(2)}) async-start(), calls=%async_computation.8 | async-start | bytes 2621440 | tf_op jit(solution)/shard_map/reduce_scatter | solution.py:256
Sparse Core Ops, SparseCore 0:
  9.2 37.2 all-gather.8
  51.7 37.5 all-gather.10
  91.1 39.5 all-gather.12
  198.1 36.0 reduce-scatter.3
  236.6 40.5 reduce-scatter.5
  284.6 35.4 reduce-scatter.7
